TPU v7x, 32 devices: a whole 2x2x4 slice. The times are simulated.
32 devices in a mesh: fsdp: 16 (over z, x, core), dp: 2 (over y).
Axes of the slice: x: 2, y: 2, z: 4, core: 2. Of those that a mesh axis runs over, the one named last changes fastest.
Arguments:
- activations: bfloat16 [8192, 4096], P(('fsdp', 'dp')), may hold values from -6 to 6
- cotangents: bfloat16 [2, 8192, 4096], P(None, ('fsdp', 'dp')), may hold values from -6 to 6
- weights: bfloat16 [2, 4096, 4096], P(None, 'fsdp'), may hold values from -4 to 4
- projectors: bfloat16 [2, 4096, 512], P(None, 'fsdp'), may hold values from -0.09375 to 0.09375
- first_moment: float32 [2, 4096, 512], P(None, 'fsdp'), may hold values from -3 to 3
- second_moment: float32 [2, 4096, 512], P(None, 'fsdp'), may hold values from 0.25 to 4
- matrix_settings: int32 [2, 2], replicated, may hold values from 0 to 512, as said below
Outputs:
- new_weights: bfloat16 [2, 4096, 4096], P(None, 'fsdp')
- new_first: float32 [2, 4096, 512], P(None, 'fsdp')
- new_second: float32 [2, 4096, 512], P(None, 'fsdp')
Inputs may be any that keep to these rules, and one draw needn't show every extreme that they name: `matrix_settings`: column 0 is a rank from 128 to 512, some matrix has rank exactly 512; column 1 is 0 (the projector acts on the activations) or 1 (on the cotangents), and both values occur.
All inputs are finite; a program needn't handle non-finite values.
Results may differ from a plain program's by a relative error of at most 0.0045.
Values may be sent and summed in bfloat16 or wider, within the bound.
A program may use at most 128 MiB of HBM per device.

v0:
```python
import math

import jax
import jax.numpy as jnp
from jax import lax
from jax.sharding import PartitionSpec as P

BETA_ONE = 0.9
BETA_TWO = 0.95
EPSILON = 1e-08


def on_device(
    activations, cotangents, weights, projectors, first_moment, second_moment, matrix_settings
):
    rank_max = projectors.shape[2]
    token_local = activations.shape[0]
    token_total = token_local * lax.axis_size("fsdp") * lax.axis_size("dp")
    grad_scale = 1.0 / math.sqrt(token_total)
    rank_columns = jnp.arange(rank_max)
    weight_list, first_list, second_list = ([], [], [])
    for matrix_index in range(cotangents.shape[0]):
        live_mask = (rank_columns < matrix_settings[matrix_index, 0])[None, :]
        on_inputs = matrix_settings[matrix_index, 1] == 0
        proj_local = jnp.where(live_mask, projectors[matrix_index], jnp.zeros((), jnp.bfloat16))
        grads_out = cotangents[matrix_index]
        projected_side = jnp.where(on_inputs, activations, grads_out)
        other_side = jnp.where(on_inputs, grads_out, activations)
        shard_piece = lax.all_gather(proj_local, "fsdp", axis=0, tiled=True)
        coeff_sum = jnp.dot(projected_side, shard_piece, preferred_element_type=jnp.float32)
        coeff_sum, full_projector = (coeff_sum, shard_piece)
        coeffs = coeff_sum.astype(jnp.bfloat16)
        regrouped = lax.all_to_all(other_side, "fsdp", split_axis=1, concat_axis=0, tiled=True)
        partial_sums = lax.dot_general(
            regrouped,
            lax.all_gather(coeffs, "fsdp", axis=0, tiled=True),
            (((0,), (0,)), ((), ())),
            preferred_element_type=jnp.float32,
        )
        projected = (
            lax.psum(partial_sums.astype(jnp.bfloat16), "dp").astype(jnp.float32) * grad_scale
        )
        moment_one = jnp.where(
            live_mask, BETA_ONE * first_moment[matrix_index] + (1.0 - BETA_ONE) * projected, 0.0
        )
        moment_two = jnp.where(
            live_mask,
            BETA_TWO * second_moment[matrix_index] + (1.0 - BETA_TWO) * projected * projected,
            0.0,
        )
        normalized = jnp.where(
            live_mask, moment_one / (jnp.sqrt(moment_two) + EPSILON), 0.0
        ).astype(jnp.bfloat16)
        update = lax.dot_general(
            normalized, full_projector, (((1,), (1,)), ((), ())), preferred_element_type=jnp.float32
        )
        weight_list.append(
            (weights[matrix_index].astype(jnp.float32) - update).astype(jnp.bfloat16)
        )
        first_list.append(moment_one)
        second_list.append(moment_two)
    return (jnp.stack(weight_list), jnp.stack(first_list), jnp.stack(second_list))


def solution(mesh):
    return jax.shard_map(
        on_device,
        mesh=mesh,
        in_specs=(
            P(("fsdp", "dp"), None),
            P(None, ("fsdp", "dp"), None),
            P(None, "fsdp", None),
            P(None, "fsdp", None),
            P(None, "fsdp", None),
            P(None, "fsdp", None),
            P(),
        ),
        out_specs=(P(None, "fsdp", None), P(None, "fsdp", None), P(None, "fsdp", None)),
        check_vma=False,
    )
```

profile of v0, /device:TPU:0, one launch (start us, length us, event | category | flops | bytes accessed | tf_op | source)
XLA Modules:
  0.0 329.5 jit_solution(16174346227881993778)
XLA Ops:
  7.2 1.5 fusion.49
  10.0 1.9 bitcast_select_fusion.11
  12.7 3.3 copy.11
  16.0 5.5 %fusion.48 = (bf16[1,256,4096]{2,1,0:T(8,128)(2,1)}, bf16[1,256,4096]{2,1,0:T(8,128)(2,1)}) fusion(bf16[2,256,4096]{2,1,0:T(8,128)(2,1)} %param.8), kind=kLoop, calls=%fused_computation.67 | loop fusion | bytes 8388608 | tf_op jit(solution)/shard_map/slice | solution.py:26
  21.4 4.1 %copy.19 = bf16[1,256,4096]{1,2,0:T(8,128)(2,1)} copy(bf16[1,256,4096]{2,1,0:T(8,128)(2,1)} %get-tuple-element.6) | data formatting | bytes 4194304
  26.2 39.1 %all-gather.9.cloned.1.call-done = bf16[4096,512]{1,0:T(8,128)(2,1)} async-done(((bf16[256,512]{1,0:T(8,128)(2,1)}), bf16[4096,512]{1,0:T(8,128)(2,1)}) %all-gather.9.cloned.1.call-update) | async-done | bytes 4194320 | tf_op jit(solution)/shard_map/all_gather | solution.py:29
  65.3 4.8 %fusion.9 = bf16[256,512]{1,0:T(8,128)(2,1)} fusion(bf16[4096,512]{1,0:T(8,128)(2,1)} %all-gather.9.cloned.1.call-done, bf16[256,4096]{0,1:T(8,128)(2,1)S(1)} %copy.11, bf16[1,256,4096]{1,2,0:T(8,128)(2,1)} %copy.19, pred[]{:T(512)} %bitcast.14), kind=kOutput, calls=%fused_computation.16 | convolution fusion | flops 1074921472 | bytes 8650753 | tf_op jit(solution)/shard_map/dot_general | solution.py:30
  70.1 4.1 %copy.18 = bf16[1,256,4096]{1,2,0:T(8,128)(2,1)} copy(bf16[1,256,4096]{2,1,0:T(8,128)(2,1)} %get-tuple-element.5) | data formatting | bytes 4194304
  74.8 4.6 %bitcast_select_fusion.4 = (bf16[256,4096]{0,1:T(8,128)(2,1)}, bf16[256,4096]{0,1:T(8,128)(2,1)}) fusion(bf16[256,4096]{0,1:T(8,128)(2,1)S(1)} %copy.11, bf16[1,256,4096]{1,2,0:T(8,128)(2,1)} %copy.18, pred[]{:T(512)} %bitcast.3, bf16[1,256,4096]{1,2,0:T(8,128)(2,1)} %copy.19, pred[]{:T(512)} %bitcast.14), kind=kLoop, calls=%fused_computation.11 | loop fusion | flops 2097152 | bytes 10485762 | tf_op jit(solution)/shard_map/jit(_where)/select_n | solution.py:28
  79.4 3.7 %all-to-all-start.1 = ((bf16[256,16,256]{0,2,1:T(8,128)(2,1)}), bf16[256,16,256]{0,2,1:T(8,128)(2,1)S(1)}, u32[]{:S(2)}, u32[]{:S(2)}) async-start(bf16[256,16,256]{0,2,1:T(8,128)(2,1)} %bitcast.82), calls=%async_computation.1 | async-start | bytes 4194304 | tf_op jit(solution)/shard_map/all_to_all | solution.py:33
  83.2 60.7 %all-gather.5.cloned.1.call-done = bf16[4096,512]{1,0:T(8,128)(2,1)} async-done(((bf16[256,512]{1,0:T(8,128)(2,1)}), bf16[4096,512]{1,0:T(8,128)(2,1)}) %all-gather.5.cloned.1.call-update) | async-done | bytes 4194320 | tf_op jit(solution)/shard_map/all_gather | solution.py:29
  143.9 5.4 %fusion.8 = bf16[256,512]{1,0:T(8,128)(2,1)} fusion(bf16[4096,512]{1,0:T(8,128)(2,1)} %all-gather.5.cloned.1.call-done, bf16[256,4096]{0,1:T(8,128)(2,1)} %copy-done, bf16[1,256,4096]{1,2,0:T(8,128)(2,1)} %copy.18, pred[]{:T(512)} %bitcast.3), kind=kOutput, calls=%fused_computation.15 | convolution fusion | flops 1074921472 | bytes 8650753 | tf_op jit(solution)/shard_map/dot_general | solution.py:30
  149.4 4.9 %all-to-all-start = ((bf16[256,16,256]{0,2,1:T(8,128)(2,1)}), bf16[256,16,256]{0,2,1:T(8,128)(2,1)}, u32[]{:S(2)}, u32[]{:S(2)}) async-start(bf16[256,16,256]{0,2,1:T(8,128)(2,1)} %bitcast.81), calls=%async_computation | async-start | bytes 4194304 | tf_op jit(solution)/shard_map/all_to_all | solution.py:33
  154.3 2.4 copy.16
  156.7 62.1 %all-to-all-done = bf16[256,16,256]{0,2,1:T(8,128)(2,1)} async-done(((bf16[256,16,256]{0,2,1:T(8,128)(2,1)}), bf16[256,16,256]{0,2,1:T(8,128)(2,1)}, u32[]{:S(2)}, u32[]{:S(2)}) %all-to-all-start) | async-done | bytes 2097184 | tf_op jit(solution)/shard_map/all_to_all | solution.py:33
  218.8 4.1 %copy.12 = bf16[16,256,256]{2,1,0:T(8,128)(2,1)} copy(bf16[16,256,256]{1,2,0:T(8,128)(2,1)} %bitcast.6) | data formatting | bytes 4194304 | tf_op jit(solution)/shard_map/all_to_all | solution.py:33
  222.8 4.2 %convolution_convert_fusion = bf16[256,512]{1,0:T(8,128)(2,1)} fusion(bf16[4096,256]{1,0:T(8,128)(2,1)S(1)} %bitcast.83, bf16[4096,512]{1,0:T(8,128)(2,1)} %all-gather.11.cloned.1.call-done), kind=kOutput, calls=%fused_computation.17 | convolution fusion | flops 1073872896 | bytes 6553600 | tf_op jit(solution)/shard_map/dot_general | solution.py:34
  227.0 51.2 %all-gather.7.cloned.1.call-done = bf16[4096,512]{1,0:T(8,128)(2,1)} async-done(((bf16[256,512]{1,0:T(8,128)(2,1)}), bf16[4096,512]{1,0:T(8,128)(2,1)}) %all-gather.7.cloned.1.call-update) | async-done | bytes 4194320 | tf_op jit(solution)/shard_map/all_gather | solution.py:36
  278.2 4.9 %convolution_convert_fusion.1 = bf16[256,512]{1,0:T(8,128)(2,1)} fusion(bf16[4096,256]{1,0:T(8,128)(2,1)} %bitcast.84, bf16[4096,512]{1,0:T(8,128)(2,1)} %all-gather.7.cloned.1.call-done), kind=kOutput, calls=%fused_computation.18 | convolution fusion | flops 1073872896 | bytes 6553600 | tf_op jit(solution)/shard_map/dot_general | solution.py:34
  283.2 27.4 %all-reduce.3.cloned.1.call-done = (bf16[256,512]{1,0:T(8,128)(2,1)}, bf16[256,512]{1,0:T(8,128)(2,1)}) async-done(((bf16[256,512]{1,0:T(8,128)(2,1)}, bf16[256,512]{1,0:T(8,128)(2,1)}), (bf16[256,512]{1,0:T(8,128)(2,1)}, bf16[256,512]{1,0:T(8,128)(2,1)})) %all-reduce.3.cloned.1.call-update) | async-done | bytes 524304 | tf_op jit(solution)/shard_map/psum | solution.py:41
  310.6 1.6 fusion.28
  313.1 3.9 %fusion.2 = bf16[1,256,4096]{2,1,0:T(8,128)(2,1)S(1)} fusion(bf16[4096,512]{1,0:T(8,128)(2,1)} %all-gather.9.cloned.1.call-done, bf16[2,256,4096]{2,1,0:T(8,128)(2,1)S(1)} %copy-done.6, pred[512]{0:T(512)(128)(4,1)S(1)} %get-tuple-element.21, bf16[256,512]{1,0:T(8,128)(2,1)S(1)} %copy-done.5, f32[2,256,512]{2,1,0:T(8,128)S(1)} %copy-done.2, ...), kind=kOutput, calls=%fused_computation.4 | convolution fusion | flops 1078853632 | bytes 9699840 | tf_op jit(solution)/shard_map/dot_general | solution.py:54
  317.0 1.5 fusion.3
  318.5 2.4 pad_maximum_fusion
  (31 shorter events, 5.2 us)
Async XLA Ops:
  7.2 58.1 %all-gather.9.cloned.1.call-start = ((), (), s32[]{:S(2)}) async-start(), calls=%async_computation.4 | async-start | bytes 4456448 | tf_op jit(solution)/shard_map/all_gather | solution.py:29
  11.9 132.0 %all-gather.5.cloned.1.call-start = ((), (), s32[]{:S(2)}) async-start(), calls=%async_computation.2 | async-start | bytes 4456448 | tf_op jit(solution)/shard_map/all_gather | solution.py:29
  12.6 210.2 %all-gather.11.cloned.1.call-start = ((), (), s32[]{:S(2)}) async-start(), calls=%async_computation.5 | async-start | bytes 4456448 | tf_op jit(solution)/shard_map/all_gather | solution.py:36
  15.9 58.9 %copy-start = (bf16[256,4096]{0,1:T(8,128)(2,1)}, bf16[256,4096]{0,1:T(8,128)(2,1)S(1)}, u32[]{:S(2)}) copy-start(bf16[256,4096]{0,1:T(8,128)(2,1)S(1)} %copy.11) | copy-start | bytes 6291460
  79.4 69.9 %all-to-all-start.1 = ((bf16[256,16,256]{0,2,1:T(8,128)(2,1)}), bf16[256,16,256]{0,2,1:T(8,128)(2,1)S(1)}, u32[]{:S(2)}, u32[]{:S(2)}) async-start(bf16[256,16,256]{0,2,1:T(8,128)(2,1)} %bitcast.82), calls=%async_computation.1 | async-start | bytes 4194304 | tf_op jit(solution)/shard_map/all_to_all | solution.py:33
  83.2 195.0 %all-gather.7.cloned.1.call-start = ((), (), s32[]{:S(2)}) async-start(), calls=%async_computation.3 | async-start | bytes 4456448 | tf_op jit(solution)/shard_map/all_gather | solution.py:36
  149.4 69.4 %all-to-all-start = ((bf16[256,16,256]{0,2,1:T(8,128)(2,1)}), bf16[256,16,256]{0,2,1:T(8,128)(2,1)}, u32[]{:S(2)}, u32[]{:S(2)}) async-start(bf16[256,16,256]{0,2,1:T(8,128)(2,1)} %bitcast.81), calls=%async_computation | async-start | bytes 4194304 | tf_op jit(solution)/shard_map/all_to_all | solution.py:33
  154.3 156.3 %all-reduce.3.cloned.1.call-start = ((), (), s32[]{:S(2)}) async-start(), calls=%async_computation.6 | async-start | bytes 1048576 | tf_op jit(solution)/shard_map/psum | solution.py:41
  218.8 4.1 %copy-start.1 = (bf16[16,256,256]{2,1,0:T(8,128)(2,1)S(1)}, bf16[16,256,256]{2,1,0:T(8,128)(2,1)}, u32[]{:S(2)}) copy-start(bf16[16,256,256]{2,1,0:T(8,128)(2,1)} %copy.16) | copy-start | bytes 6291460
  278.2 32.4 %copy-start.2 = (f32[2,256,512]{2,1,0:T(8,128)S(1)}, f32[2,256,512]{2,1,0:T(8,128)}, u32[]{:S(2)}) copy-start(f32[2,256,512]{2,1,0:T(8,128)} %param.11) | copy-start | bytes 3145732
  278.2 32.4 %copy-start.3 = (f32[2,256,512]{2,1,0:T(8,128)S(1)}, f32[2,256,512]{2,1,0:T(8,128)}, u32[]{:S(2)}) copy-start(f32[2,256,512]{2,1,0:T(8,128)} %param.12) | copy-start | bytes 3145732
  310.6 1.6 copy-start.5
  310.6 2.4 copy-start.6
  313.1 3.9 %copy-start.4 = (bf16[256,512]{1,0:T(8,128)(2,1)S(1)}, bf16[256,512]{1,0:T(8,128)(2,1)}, u32[]{:S(2)}) copy-start(bf16[256,512]{1,0:T(8,128)(2,1)} %get-tuple-element.4) | copy-start | bytes 786436
  313.1 3.9 %copy-start.7 = (bf16[4096,512]{1,0:T(8,128)(2,1)S(1)}, bf16[4096,512]{1,0:T(8,128)(2,1)}, u32[]{:S(2)}) copy-start(bf16[4096,512]{1,0:T(8,128)(2,1)} %all-gather.5.cloned.1.call-done) | copy-start | bytes 12582916
Sparse Core Ops, SparseCore 0:
  12.0 53.2 all-gather.8
  68.0 75.8 all-gather.4
  146.6 75.3 all-gather.10
  224.1 54.0 all-gather.6
  283.3 27.2 all-reduce.2
where the time goes:
time: 330 us; the launch traced here: 329 us
  waiting for transfers between devices  241 us (73%)
  local copies, waits for them, and re-layouts  25.8 us (8%)
  matrix products  24.8 us (8%)
  between operations  15.1 us (5%)
  other arithmetic  13.8 us (4%)
  starting transfers between devices  8.8 us (3%)
    all_gather x2, waiting for transfers between devices, on_device(): shard_piece = lax.all_gather(proj_local, 'fsdp', axis=0, tiled=True)  99.8 us
    all_to_all x2, waiting for transfers between devices, on_device(): lax.all_to_all(other_side, 'fsdp', split_axis=1, concat_axis=0, tiled=True)  62.1 us
    all_gather x2, waiting for transfers between devices, on_device(): lax.all_gather(coeffs, 'fsdp', axis=0, tiled=True)  51.2 us
    psum x1, waiting for transfers between devices, on_device(): lax.psum(partial_sums.astype(jnp.bfloat16), 'dp').astype(jnp.float32)  27.4 us
    unnamed x19, local copies, waits for them, and re-layouts  12.3 us
    dot_general x2, matrix products, on_device(): jnp.dot(projected_side, shard_piece, preferred_element_type=jnp.float32)  10.2 us
    dot_general x2, matrix products, on_device(): lax.dot_general(regrouped, lax.all_gather(coeffs, 'fsdp', axis=0, tiled=T...  9.09 us
    all_to_all x2, starting transfers between devices, on_device(): lax.all_to_all(other_side, 'fsdp', split_axis=1, concat_axis=0, tiled=True)  8.6 us
  transfers between devices with their start and end apart: 7, of which 5 were waited for; matrix products, arithmetic and copies ran while one was open for 13% of the time, Pallas kernels for 0%

commit v1 on v0

v1 whole, which is shorter than its diff:
```python
import functools
import math

import jax
import jax.numpy as jnp
from jax import lax
from jax.experimental import pallas as pl
from jax.experimental.pallas import tpu as pltpu
from jax.sharding import PartitionSpec as P

BETA_ONE = 0.9
BETA_TWO = 0.95
EPSILON = 1e-08
MESH = pl.DeviceIdType.MESH
BF16, F32 = jnp.bfloat16, jnp.float32


def split_axis(fsdp):
    chips = fsdp // 2
    inner = 1
    while (2 * inner) ** 2 <= chips and chips % (2 * inner) == 0:
        inner *= 2
    return chips // inner, inner


def shared_rows(rows, dp):
    return (rows * 3 // 8) // 32 * 32 if dp == 2 else 0


def kernel(
    fsdp, dp, scale,
    settings, act, cot, wts, prj, mom1, mom2, w_out, m1_out, m2_out,
    xs, proj, own_t, sib_t, send_t, own_c, sib_c, acc, zacc, xsend, xrecv, zsend, zrecv, ybuf, wbuf, m1, m2, nbuf,
    in_sem, out_sem, gz, gx, gy, gs, st, sc, rx, rz, ry,
):
    mats, _, rows, rank_max = proj.shape
    tokens = act.shape[0]
    outer, inner = split_axis(fsdp)
    chips = outer * inner
    me, my_dp = lax.axis_index("fsdp"), lax.axis_index("dp")
    core = lax.rem(me, 2)
    chip = me // 2
    my_x, my_z = lax.rem(chip, inner), chip // inner
    sibling = chip * 2 + 1 - core

    def chip_at(dz, dx):
        return lax.rem(my_z + dz + outer, outer) * inner + lax.rem(my_x + dx + inner, inner)

    def dev_at(dz, dx):
        return chip_at(dz, dx) * 2 + core

    sent = []

    def copy(src, dst, sems, index, device):
        return pltpu.make_async_remote_copy(
            src_ref=src,
            dst_ref=dst,
            send_sem=sems.at[(0, *index)],
            recv_sem=sems.at[(1, *index)],
            device_id=device,
            device_id_type=MESH,
        )

    def start(*args):
        one = copy(*args)
        one.start()
        sent.append(one)

    loads = [
        pltpu.make_async_copy(prj, proj.at[:, me], in_sem.at[0]),
        pltpu.make_async_copy(act, xs.at[0], in_sem.at[1]),
        pltpu.make_async_copy(cot, xs.at[pl.ds(1, mats)], in_sem.at[2]),
        pltpu.make_async_copy(mom1, m1, in_sem.at[3]),
        pltpu.make_async_copy(mom2, m2, in_sem.at[4]),
        pltpu.make_async_copy(wts, wbuf, in_sem.at[5]),
    ]
    for one in loads:
        one.start()

    partners = [{"fsdp": sibling}]
    partners += [{"fsdp": dev_at(0, e)} for e in range(1, inner)]
    partners += [{"fsdp": dev_at(d, 0)} for d in range(1, outer)]
    partners += [{"dp": lax.rem(my_dp + s, dp)} for s in range(1, dp)]
    barrier = pltpu.get_barrier_semaphore()
    for partner in partners:
        pl.semaphore_signal(barrier, inc=1, device_id=partner, device_id_type=MESH)
    pl.semaphore_wait(barrier, len(partners))
    loads[0].wait()

    share = shared_rows(rows, dp)
    window = rows - share
    half = window // 2
    window_at = my_dp * share

    def piece(k, owner, h):
        return proj.at[k, owner, pl.ds(pl.multiple_of(window_at + h * half, 16), half)]

    def y_piece(k, owner, plane):
        return proj.at[k, owner, pl.ds(pl.multiple_of(plane * window, 16), share)]

    def z_start(k, h):
        for d in range(1, outer):
            start(piece(k, me, h), piece(k, me, h), gz, (k, h, d - 1), {"fsdp": dev_at(d, 0)})

    def x_start(k, h, d):
        owner = dev_at(-d, 0)
        for e in range(1, inner):
            start(piece(k, owner, h), piece(k, owner, h), gx, (k, h, d, e - 1), {"fsdp": dev_at(0, e)})

    def z_forward(k, h):
        for d in range(1, outer):
            got = piece(k, dev_at(-d, 0), h)
            copy(got, got, gz, (k, h, d - 1), {"fsdp": dev_at(-d, 0)}).wait_recv()
            x_start(k, h, d)

    def y_start(k, d, e):
        if share:
            part = y_piece(k, dev_at(-d, -e), my_dp)
            start(part, part, gy, (k, d, e), {"dp": 1 - my_dp})

    def x_arrived(k, y_too=True):
        for d in range(outer):
            for e in range(1, inner):
                for h in range(2):
                    got = piece(k, dev_at(-d, -e), h)
                    copy(got, got, gx, (k, h, d, e - 1), {"fsdp": dev_at(0, -e)}).wait_recv()
                y_start(k, d, e)

    def to_sibling(k):
        for d in range(outer):
            for e in range(inner):
                owner = dev_at(-d, -e)
                if share and (d or e):
                    got = y_piece(k, owner, 1 - my_dp)
                    copy(got, got, gy, (k, d, e), {"dp": 1 - my_dp}).wait_recv()
                block = proj.at[k, owner]
                start(block, block, gs, (k, d, e), {"fsdp": sibling})

    def from_sibling(k):
        for d in range(outer):
            for e in range(inner):
                block = proj.at[k, chip_at(-d, -e) * 2 + 1 - core]
                copy(block, block, gs, (k, d, e), {"fsdp": sibling}).wait_recv()

    z_start(0, 0)
    x_start(0, 0, 0)
    z_start(0, 1)
    x_start(0, 1, 0)

    loads[1].wait()
    loads[2].wait()

    def columns(f):
        return pl.ds(pl.multiple_of(f * rows, rows), rows)

    def stage(k):
        other = jnp.where(settings[k, 1] == 0, 1 + k, 0)

        def body(c, carry):
            own_t[k, c] = xs[other, :, columns(c * 2 + core)].T
            send_t[k, c] = xs[other, :, columns(c * 2 + 1 - core)].T
            return carry

        lax.fori_loop(0, chips, body, 0)
        start(send_t.at[k], sib_t.at[k], st, (k,), {"fsdp": sibling})

    for k in range(mats):
        stage(k)

    z_forward(0, 0)
    z_start(1, 0)
    x_start(1, 0, 0)
    z_forward(0, 1)
    for d in range(1, outer):
        y_start(0, d, 0)
    z_start(1, 1)
    x_start(1, 1, 0)
    x_arrived(0)
    z_forward(1, 0)
    to_sibling(0)
    z_forward(1, 1)
    for d in range(1, outer):
        y_start(1, d, 0)
    from_sibling(0)

    def coefficients(k):
        projected = jnp.where(settings[k, 1] == 0, 0, 1 + k)
        acc[...] = jnp.zeros_like(acc)

        def body(f, carry):
            acc[...] += jnp.dot(xs[projected, :, columns(f)], proj[k, f], preferred_element_type=F32)
            return carry

        lax.fori_loop(0, fsdp, body, 0)
        own_c[k] = acc[...].astype(BF16)
        start(own_c.at[k], sib_c.at[k], sc, (k,), {"fsdp": sibling})

    def share_arrived(k):
        copy(own_c.at[k], sib_c.at[k], sc, (k,), {"fsdp": sibling}).wait_recv()
        copy(send_t.at[k], sib_t.at[k], st, (k,), {"fsdp": sibling}).wait_recv()

    order = list(range(1, outer)) + [0]

    def partial(k, c):
        return jnp.dot(own_t[k, c], own_c[k], preferred_element_type=F32) + jnp.dot(
            sib_t[k, c], sib_c[k], preferred_element_type=F32
        )

    def reduce_x(k):
        for d in order:
            for e in range(1, inner):
                xsend[k, d, e - 1] = partial(k, chip_at(d, e)).astype(BF16)
                start(xsend.at[k, d, e - 1], xrecv.at[k, d, e - 1], rx, (k, d, e - 1), {"fsdp": dev_at(0, e)})

    def reduce_z(k):
        for d in order:
            total = partial(k, chip_at(d, 0))
            for e in range(1, inner):
                copy(xsend.at[k, d, e - 1], xrecv.at[k, d, e - 1], rx, (k, d, e - 1), {"fsdp": dev_at(0, e)}).wait_recv()
                total += xrecv[k, d, e - 1].astype(F32)
            if d:
                zsend[k, d - 1] = total.astype(BF16)
                start(zsend.at[k, d - 1], zrecv.at[k, d - 1], rz, (k, d - 1), {"fsdp": dev_at(d, 0)})
            else:
                zacc[k] = total

    def reduce_y(k):
        for d in range(1, outer):
            copy(zsend.at[k, d - 1], zrecv.at[k, d - 1], rz, (k, d - 1), {"fsdp": dev_at(d, 0)}).wait_recv()
        total = zacc[k]
        for d in range(1, outer):
            total += zrecv[k, d - 1].astype(F32)
        ybuf[k, my_dp] = total.astype(BF16)
        for s in range(1, dp):
            start(ybuf.at[k, my_dp], ybuf.at[k, my_dp], ry, (k, s - 1), {"dp": lax.rem(my_dp + s, dp)})

    def finish(k):
        for s in range(1, dp):
            got = ybuf.at[k, lax.rem(my_dp - s + dp, dp)]
            copy(got, got, ry, (k, s - 1), {"dp": lax.rem(my_dp + s, dp)}).wait_recv()
        live = lax.broadcasted_iota(jnp.int32, (rows, rank_max), 1) < settings[k, 0]
        total = ybuf[k, 0].astype(F32)
        for s in range(1, dp):
            total += ybuf[k, s].astype(F32)
        grad = total * scale
        first = jnp.where(live, BETA_ONE * m1[k] + (1.0 - BETA_ONE) * grad, 0.0)
        second = jnp.where(live, BETA_TWO * m2[k] + (1.0 - BETA_TWO) * grad * grad, 0.0)
        m1[k] = first
        m2[k] = second
        pltpu.make_async_copy(m1.at[k], m1_out.at[k], out_sem.at[0, k]).start()
        pltpu.make_async_copy(m2.at[k], m2_out.at[k], out_sem.at[1, k]).start()
        nbuf[...] = jnp.where(live, first / (jnp.sqrt(second) + EPSILON), 0.0).astype(BF16)

        def body(f, carry):
            update = lax.dot_general(
                nbuf[...], proj[k, f], (((1,), (1,)), ((), ())), preferred_element_type=F32
            )
            wbuf[k, :, columns(f)] = (wbuf[k, :, columns(f)].astype(F32) - update).astype(BF16)
            return carry

        lax.fori_loop(0, fsdp, body, 0)
        pltpu.make_async_copy(wbuf.at[k], w_out.at[k], out_sem.at[2, k]).start()

    coefficients(0)
    share_arrived(0)
    x_arrived(1)
    reduce_x(0)
    to_sibling(1)
    reduce_z(0)
    from_sibling(1)
    coefficients(1)
    share_arrived(1)
    reduce_x(1)
    reduce_y(0)
    reduce_z(1)
    for one in loads[3:]:
        one.wait()
    finish(0)
    reduce_y(1)
    finish(1)

    for k in range(mats):
        pltpu.make_async_copy(m1.at[k], m1_out.at[k], out_sem.at[0, k]).wait()
        pltpu.make_async_copy(m2.at[k], m2_out.at[k], out_sem.at[1, k]).wait()
        pltpu.make_async_copy(wbuf.at[k], w_out.at[k], out_sem.at[2, k]).wait()
    for one in sent:
        one.wait_send()


def on_device(fsdp, dp, activations, cotangents, weights, projectors, first_moment, second_moment, matrix_settings):
    tokens, features = activations.shape
    mats, rows, rank_max = projectors.shape
    outer, inner = split_axis(fsdp)
    chips = outer * inner
    scale = 1.0 / math.sqrt(tokens * fsdp * dp)
    hbm = pl.BlockSpec(memory_space=pl.ANY)
    sems = pltpu.SemaphoreType.DMA
    flops = 2 * mats * features * rank_max * (2 * tokens + rows) + 2 * mats * tokens * features * rank_max
    return pl.pallas_call(
        functools.partial(kernel, fsdp, dp, scale),
        out_shape=(
            jax.ShapeDtypeStruct(weights.shape, weights.dtype),
            jax.ShapeDtypeStruct(first_moment.shape, first_moment.dtype),
            jax.ShapeDtypeStruct(second_moment.shape, second_moment.dtype),
        ),
        in_specs=[pl.BlockSpec(memory_space=pltpu.SMEM)] + [hbm] * 6,
        out_specs=(hbm, hbm, hbm),
        scratch_shapes=[
            pltpu.VMEM((mats + 1, tokens, features), BF16),
            pltpu.VMEM((mats, fsdp, rows, rank_max), BF16),
            pltpu.VMEM((mats, chips, rows, tokens), BF16),
            pltpu.VMEM((mats, chips, rows, tokens), BF16),
            pltpu.VMEM((mats, chips, rows, tokens), BF16),
            pltpu.VMEM((mats, tokens, rank_max), BF16),
            pltpu.VMEM((mats, tokens, rank_max), BF16),
            pltpu.VMEM((tokens, rank_max), F32),
            pltpu.VMEM((mats, rows, rank_max), F32),
            pltpu.VMEM((mats, outer, inner - 1, rows, rank_max), BF16),
            pltpu.VMEM((mats, outer, inner - 1, rows, rank_max), BF16),
            pltpu.VMEM((mats, outer - 1, rows, rank_max), BF16),
            pltpu.VMEM((mats, outer - 1, rows, rank_max), BF16),
            pltpu.VMEM((mats, dp, rows, rank_max), BF16),
            pltpu.VMEM((mats, rows, features), BF16),
            pltpu.VMEM((mats, rows, rank_max), F32),
            pltpu.VMEM((mats, rows, rank_max), F32),
            pltpu.VMEM((rows, rank_max), BF16),
            sems((6,)),
            sems((3, mats)),
            sems((2, mats, 2, outer - 1)),
            sems((2, mats, 2, outer, inner - 1)),
            sems((2, mats, outer, inner)),
            sems((2, mats, outer, inner)),
            sems((2, mats)),
            sems((2, mats)),
            sems((2, mats, outer, inner - 1)),
            sems((2, mats, outer - 1)),
            sems((2, mats, dp - 1)),
        ],
        compiler_params=pltpu.CompilerParams(
            collective_id=0, has_side_effects=True, vmem_limit_bytes=56 * 1024 * 1024
        ),
        cost_estimate=pl.CostEstimate(flops=flops, bytes_accessed=24 * 1024 * 1024, transcendentals=0),
    )(matrix_settings, activations, cotangents, weights, projectors, first_moment, second_moment)


def solution(mesh):
    return jax.shard_map(
        functools.partial(on_device, mesh.shape["fsdp"], mesh.shape["dp"]),
        mesh=mesh,
        in_specs=(
            P(("fsdp", "dp"), None),
            P(None, ("fsdp", "dp"), None),
            P(None, "fsdp", None),
            P(None, "fsdp", None),
            P(None, "fsdp", None),
            P(None, "fsdp", None),
            P(),
        ),
        out_specs=(P(None, "fsdp", None), P(None, "fsdp", None), P(None, "fsdp", None)),
        check_vma=False,
    )
```

time: 330 us -> 130 us (0.39)
  the two profiles are of different devices: /device:TPU:0 before, /device:TPU:31 now
where the time goes in v1:
time: 130 us; the launch traced here: 129 us
  Pallas kernels  122 us (94%)
  local copies, waits for them, and re-layouts  6.79 us (5%)
    pallas_call x1, Pallas kernels, on_device(): pl.pallas_call(functools.partial(kernel, fsdp, dp, scale), out_shape=(jax...  122 us
    unnamed x7, local copies, waits for them, and re-layouts  6.79 us

profile of v1, /device:TPU:31, one launch (start us, length us, event | category | flops | bytes accessed | tf_op | source)
XLA Modules:
  0.0 129.4 jit_solution(9390609208690966182)
XLA Ops:
  0.6 121.9 %shard_map.94 = (bf16[2,256,4096]{2,1,0:T(8,128)(2,1)}, f32[2,256,512]{2,1,0:T(8,128)}, f32[2,256,512]{2,1,0:T(8,128)}) custom-call(s32[2,2]{1,0:T(2,128)} %settings.1, bf16[256,4096]{1,0:T(8,128)(2,1)} %act.1, bf16[2,256,4096]{2,1,0:T(8,128)(2,1)} %cot.1, bf16[2,256,4096]{2,1,0:T(8,128)(2,1)} %wts.1, bf16[2,256,512]{2,1,0:T(8,128)(2,1)} %prj.1, ...), custom_call_target="tpu_custom_call" | custom-call | flops 8589934592 | bytes 25165824 | tf_op jit(solution)/shard_map/pallas_call | solution.py:299
  122.5 0.0 copy-start.1
  122.6 0.0 copy-start
  122.6 4.8 %copy.13 = bf16[2,256,4096]{2,1,0:T(8,128)(2,1)} copy(bf16[2,256,4096]{2,1,0:T(8,128)(2,1)} %get-tuple-element.6) | data formatting | bytes 8388608
  127.4 0.0 copy-done.1
  127.4 1.0 copy.14
  128.4 0.0 copy-done
  128.4 1.0 copy.15
Async XLA Ops:
  122.5 4.9 %copy-start.1 = (f32[2,256,512]{2,1,0:T(8,128)S(1)}, f32[2,256,512]{2,1,0:T(8,128)}, u32[]{:S(2)}) copy-start(f32[2,256,512]{2,1,0:T(8,128)} %get-tuple-element.7) | copy-start | bytes 3145732
  122.6 5.8 %copy-start = (f32[2,256,512]{2,1,0:T(8,128)S(1)}, f32[2,256,512]{2,1,0:T(8,128)}, u32[]{:S(2)}) copy-start(f32[2,256,512]{2,1,0:T(8,128)} %get-tuple-element.8) | copy-start | bytes 3145732
